TPU v7x, 1024 devices: a whole 8x8x8 slice. The times are simulated.
1024 devices in a mesh: dp: 128 (over z, y, x_hi), tensor: 8 (over x_lo, core).
Axes of the slice: x: 8 (x_hi: 2, x_lo: 4; x = x_hi * 4 + x_lo), y: 8, z: 8, core: 2. Of those that a mesh axis runs over, the one named last changes fastest.
Arguments:
- queries: bfloat16 [512, 96, 8192], P('dp', None, 'tensor'), may hold values from -6 to 6
- keys: bfloat16 [512, 96, 1024], P('dp', None, 'tensor'), may hold values from -6 to 6
- values: bfloat16 [512, 96, 1024], P('dp', None, 'tensor'), may hold values from -6 to 6
- hidden: bfloat16 [512, 96, 5120], P('dp', None, 'tensor'), may hold values from -6 to 6
- grad_out: bfloat16 [512, 96, 8192], P('dp', None, 'tensor'), may hold values from -6 to 6
- group_alive: int32 [256], replicated, may hold values from 0 to 1, as said below
- positions: int32 [512, 96], P('dp'), may hold values from -47 to 95, as said below
Outputs:
- grad_queries: bfloat16 [512, 96, 8192], P('dp', None, 'tensor')
- grad_keys: bfloat16 [512, 96, 1024], P('dp', None, 'tensor')
- grad_weight: float32 [1024, 5120], P('dp', 'tensor')
Inputs may be any that keep to these rules, and one draw needn't show every extreme that they name: `group_alive`: index i and index i + 64 of dp form a pair holding 2 * 2 rollout groups; in each pair exactly one of them has 0. Along a row the positions rise by one from a start of 0 or below.
All inputs are finite; a program needn't handle non-finite values.
Results may differ from a plain program's by a relative error of at most 0.0064.
Values may be sent and summed in bfloat16 or wider, within the bound.
A program may use at most 32 MiB of HBM per device.

v0:
```python
import jax
import jax.numpy as jnp
from jax import lax
from jax.sharding import PartitionSpec as P

HD = 128
GROUP = 2
CAP = 3


def partner(value, axis, distance):
    return lax.ppermute(value, axis, [(i, i ^ 1 << distance) for i in range(lax.axis_size(axis))])


def attend(query_rows, key_rows, value_rows, grad_rows, key_valid):
    length = query_rows.shape[0]
    kv_heads = key_rows.shape[-1] // HD
    q_group = query_rows.shape[-1] // HD // kv_heads
    query_b = query_rows.reshape(length, kv_heads, q_group, HD)
    key_b = key_rows.reshape(length, kv_heads, HD)
    value_b = value_rows.reshape(length, kv_heads, HD)
    grad_b = grad_rows.reshape(length, kv_heads, q_group, HD)
    factor = HD ** (-0.5)
    scores = (
        jnp.einsum("qhgd,khd->hgqk", query_b, key_b, preferred_element_type=jnp.float32) * factor
    )
    q_index = jnp.arange(length)[:, None]
    k_index = jnp.arange(length)[None, :]
    allowed = (k_index <= q_index) & ((key_valid[None, :] > 0) | (k_index == q_index))
    scores = jnp.where(allowed, scores, jnp.float32(-1e30))
    top_score = jnp.max(scores, axis=-1, keepdims=True)
    expo = jnp.exp(scores - top_score)
    probs = expo / jnp.sum(expo, axis=-1, keepdims=True)
    probs_half = probs.astype(jnp.bfloat16)
    attended = jnp.einsum("hgqk,khd->qhgd", probs_half, value_b, preferred_element_type=jnp.float32)
    delta = jnp.transpose(jnp.sum(grad_b.astype(jnp.float32) * attended, axis=-1), (1, 2, 0))
    dprobs = jnp.einsum("qhgd,khd->hgqk", grad_b, value_b, preferred_element_type=jnp.float32)
    dscores_half = (probs * (dprobs - delta[..., None])).astype(jnp.bfloat16)
    grad_query = (
        jnp.einsum("hgqk,khd->qhgd", dscores_half, key_b, preferred_element_type=jnp.float32)
        * factor
    )
    grad_key = (
        jnp.einsum("hgqk,qhgd->khd", dscores_half, query_b, preferred_element_type=jnp.float32)
        * factor
    )
    grad_value = jnp.einsum(
        "hgqk,qhgd->khd", probs_half, grad_b, preferred_element_type=jnp.float32
    )
    return (
        grad_query.reshape(length, -1),
        grad_key.reshape(length, -1),
        grad_value.reshape(length, -1),
    )


def pair_slots(group_alive, lower_index, half_count, parity, per_device):
    lower_groups = lax.dynamic_slice_in_dim(group_alive, lower_index * per_device, per_device)
    upper_groups = lax.dynamic_slice_in_dim(
        group_alive, (lower_index + half_count) * per_device, per_device
    )
    rows_alive = jnp.repeat(jnp.concatenate([lower_groups, upper_groups], 0), GROUP)
    rank = jnp.cumsum(rows_alive) - 1
    target = 2 * jnp.arange(CAP, dtype=jnp.int32)[:, None] + parity
    hit = (rows_alive[None, :] > 0) & (rank[None, :] == target)
    numbers = jnp.arange(rows_alive.shape[0], dtype=jnp.int32)[None, :]
    return jnp.sum(jnp.where(hit, numbers, 0), axis=1)


def local(queries, keys, values, hidden, grad_out, group_alive, positions):
    row_count = queries.shape[0]
    per_device = row_count // GROUP
    half_count = lax.axis_size("dp") // 2
    top_bit = lax.axis_size("dp").bit_length() - 2
    my_index = lax.axis_index("dp")
    is_upper = my_index // half_count
    lower_index = my_index % half_count
    offset = is_upper * row_count
    my_groups = lax.dynamic_slice_in_dim(group_alive, my_index * per_device, per_device)
    alive_row = jnp.repeat(my_groups, GROUP)
    masked = grad_out * alive_row.astype(grad_out.dtype)[:, None, None]
    key_valid = (positions >= 0).astype(jnp.bfloat16)
    my_slots = pair_slots(group_alive, lower_index, half_count, is_upper, per_device)
    far_slots = pair_slots(group_alive, lower_index, half_count, 1 - is_upper, per_device)
    own_rows = (queries, keys, values, masked, key_valid)
    far_rows = partner((queries, keys, values, masked, key_valid), "dp", top_bit)

    def choose_row(local_part, remote_part):
        paired = jnp.where(
            is_upper == 1,
            jnp.concatenate([remote_part, local_part], 0),
            jnp.concatenate([local_part, remote_part], 0),
        )
        return jnp.take(paired, my_slots, axis=0)

    chosen = tuple(
        (choose_row(local_part, remote_part) for local_part, remote_part in zip(own_rows, far_rows))
    )
    grad_query, grad_key, grad_value = jax.vmap(attend)(*chosen)
    computed = (
        grad_query.astype(jnp.bfloat16),
        grad_key.astype(jnp.bfloat16),
        grad_value.astype(jnp.bfloat16),
    )
    returned = partner((computed[0], computed[1], computed[2]), "dp", top_bit)
    home_index = jnp.arange(row_count)
    from_mine = ((my_slots - offset)[None, :] == home_index[:, None]).astype(jnp.float32)
    from_far = ((far_slots - offset)[None, :] == home_index[:, None]).astype(jnp.float32)

    def place_home(local_part, remote_part):
        summed = jnp.einsum("hc,clx->hlx", from_mine, local_part.astype(jnp.float32)) + jnp.einsum(
            "hc,clx->hlx", from_far, remote_part.astype(jnp.float32)
        )
        return summed.astype(jnp.bfloat16)

    home_query = place_home(computed[0], returned[0])
    home_key = place_home(computed[1], returned[1])
    home_value = place_home(computed[2], returned[2])
    token_count = home_value.shape[0] * home_value.shape[1]
    value_flat = home_value.reshape(token_count, -1)
    hidden_flat = hidden.reshape(token_count, -1)
    value_all = lax.all_gather(value_flat, "tensor", axis=1, tiled=True)
    grad_weight = lax.psum_scatter(
        lax.dot_general(
            value_all, hidden_flat, (((0,), (0,)), ((), ())), preferred_element_type=jnp.float32
        ),
        "dp",
        scatter_dimension=0,
        tiled=True,
    )
    return (home_query, home_key, grad_weight)


def solution(mesh):
    return jax.shard_map(
        local,
        mesh=mesh,
        in_specs=(
            P("dp", None, "tensor"),
            P("dp", None, "tensor"),
            P("dp", None, "tensor"),
            P("dp", None, "tensor"),
            P("dp", None, "tensor"),
            P(),
            P("dp", None),
        ),
        out_specs=(P("dp", None, "tensor"), P("dp", None, "tensor"), P("dp", "tensor")),
        check_vma=False,
    )
```

profile of v0, /device:TPU:8, one launch (start us, length us, event | category | flops | bytes accessed | tf_op | source)
XLA Modules:
  0.0 1797.5 jit_solution(1962590378735360537)
XLA Ops:
  7.2 14.7 collective-permute-start
  22.6 1.9 collective-permute-start.1
  24.5 7.8 collective-permute-start.2
  33.4 1.3 broadcast_multiply_fusion
  34.7 1.9 collective-permute-start.4
  40.0 11.3 collective-permute-done.2
  51.3 2.2 maximum_select_fusion
  54.2 12.5 collective-permute-done.4
  66.7 1.6 maximum_select_fusion.1
  70.6 1.1 copy.67
  73.2 41.2 %collective-permute-start.7 = (bf16[3,96,128]{2,1,0:T(8,128)(2,1)S(1)}, bf16[3,96,128]{2,1,0:T(8,128)(2,1)S(1)}, u32[]{:S(2)}, u32[]{:S(2)}) collective-permute-start(bf16[3,96,128]{2,1,0:T(8,128)(2,1)S(1)} %fusion.15), channel_id=1, source_target_pairs={{0,512},{8,520},{16,528},{24,536},{32,544},{40,552},{48,560},{56,5... | collective-permute-start | bytes 221192 | tf_op jit(solution)/shard_map/ppermute | solution.py:12
  114.6 2.5 collective-permute-done.7
  117.3 15.0 all_gather.3
  132.3 2.5 fusion.55
  134.8 8.3 collective-permute-start.3
  143.1 1.3 dynamic-slice
  145.0 1.8 collective-permute-done.3
  146.8 1.7 maximum_select_fusion.3
  148.5 2.2 gather_fusion.3
  154.2 9.4 collective-permute-start.5
  164.7 1.9 collective-permute-start.6
  166.8 9.8 collective-permute-done.6
  179.4 1610.0 %all-reduce.3.cloned.1.call-done = f32[1024,640]{1,0:T(8,128)} async-done(((f32[1024,640]{1,0:T(8,128)}), f32[1024,640]{1,0:T(8,128)}) %all-reduce.3.cloned.1.call-update) | async-done | bytes 2621456
  1789.3 1.3 constant_dynamic-slice_fusion
  (75 shorter events, 17.2 us)
Async XLA Ops:
  7.2 125.1 %copy-start = (bf16[4,96,640]{2,1,0:T(8,128)(2,1)S(1)}, bf16[4,96,640]{2,1,0:T(8,128)(2,1)}, u32[]{:S(2)}) copy-start(bf16[4,96,640]{2,1,0:T(8,128)(2,1)} %param.14) | copy-start | bytes 1474564
  7.2 32.2 %copy-start.5 = (bf16[4,96,128]{2,1,0:T(8,128)(2,1)S(1)}, bf16[4,96,128]{2,1,0:T(8,128)(2,1)}, u32[]{:S(2)}) copy-start(bf16[4,96,128]{2,1,0:T(8,128)(2,1)} %param.12) | copy-start | bytes 294916
  7.2 1782.1 %all-reduce.3.cloned.1.call-start = ((), (), s32[]{:S(2)}) async-start(), calls=%async_computation | async-start | bytes 5242880
  7.2 32.1 %collective-permute-start = (bf16[4,96,128]{2,1,0:T(8,128)(2,1)}, bf16[4,96,128]{2,1,0:T(8,128)(2,1)S(1)}, u32[]{:S(2)}, u32[]{:S(2)}) collective-permute-start(bf16[4,96,128]{2,1,0:T(8,128)(2,1)} %param.12), channel_id=1, source_target_pairs={{0,512},{8,520},{16,528},{24,536},{32,544},{40,552},{48,560},{56,5... | collective-permute-start | bytes 294920 | tf_op jit(solution)/shard_map/ppermute | solution.py:12
  22.6 16.0 collective-permute-start.1
  24.5 26.7 %collective-permute-start.2 = (bf16[4,96,1024]{2,1,0:T(8,128)(2,1)}, bf16[4,96,1024]{2,1,0:T(8,128)(2,1)}, u32[]{:S(2)}, u32[]{:S(2)}) collective-permute-start(bf16[4,96,1024]{2,1,0:T(8,128)(2,1)} %param.11), channel_id=1, source_target_pairs={{0,512},{8,520},{16,528},{24,536},{32,544},{40,552},{48,560},{56,5... | collective-permute-start | bytes 2359304 | tf_op jit(solution)/shard_map/ppermute | solution.py:12
  34.7 32.0 %collective-permute-start.4 = (bf16[4,96,1024]{2,1,0:T(8,128)(2,1)S(1)}, bf16[4,96,1024]{2,1,0:T(8,128)(2,1)}, u32[]{:S(2)}, u32[]{:S(2)}) collective-permute-start(bf16[4,96,1024]{2,1,0:T(8,128)(2,1)S(1)} %broadcast_multiply_fusion), channel_id=1, source_target_pairs={{0,512},{8,520},{16,528},{24,536},{32,544},{40,552},{48,560},{56,5... | collective-permute-start | bytes 2359304 | tf_op jit(solution)/shard_map/ppermute | solution.py:12
  38.0 1.9 copy-start.6
  69.8 0.6 copy-start.3
  71.8 1.1 copy-start.1
  71.8 42.7 %copy-start.7 = (s32[3]{0:T(128)S(1)}, s32[3]{0:T(128)}, u32[]{:S(2)}) copy-start(s32[3]{0:T(128)} %get-tuple-element.24) | copy-start | bytes 40
  71.8 45.3 %copy-start.8 = (s32[3]{0:T(128)S(1)}, s32[3]{0:T(128)}, u32[]{:S(2)}) copy-start(s32[3]{0:T(128)} %broadcast_subtract_fusion) | copy-start | bytes 40
  73.2 43.9 %collective-permute-start.7 = (bf16[3,96,128]{2,1,0:T(8,128)(2,1)S(1)}, bf16[3,96,128]{2,1,0:T(8,128)(2,1)S(1)}, u32[]{:S(2)}, u32[]{:S(2)}) collective-permute-start(bf16[3,96,128]{2,1,0:T(8,128)(2,1)S(1)} %fusion.15), channel_id=1, source_target_pairs={{0,512},{8,520},{16,528},{24,536},{32,544},{40,552},{48,560},{56,5... | collective-permute-start | bytes 221192 | tf_op jit(solution)/shard_map/ppermute | solution.py:12
  134.8 12.0 collective-permute-start.3
  150.8 0.9 copy-start.2
  150.9 1.5 copy-start.4
  154.2 23.3 %collective-permute-start.5 = (bf16[3,96,1024]{2,1,0:T(8,128)(2,1)S(1)}, bf16[3,96,1024]{2,1,0:T(8,128)(2,1)S(1)}, u32[]{:S(2)}, u32[]{:S(2)}) collective-permute-start(bf16[3,96,1024]{2,1,0:T(8,128)(2,1)S(1)} %convert_element_type.97), channel_id=1, source_target_pairs={{0,512},{8,520},{16,528},{24,536},{32,544},{40,552},{48,560},{56,5... | collective-permute-start | bytes 1769480 | tf_op jit(solution)/shard_map/ppermute | solution.py:12
  164.7 11.9 collective-permute-start.6
Sparse Core Ops, SparseCore 0:
  134.9 1654.3 all-reduce.2
where the time goes:
time: 1800 us
  waiting for transfers between devices  1650 us (92%)
  starting transfers between devices  87.2 us (5%)
    unnamed x2, waiting for transfers between devices  1610 us
    ppermute x8, starting transfers between devices, partner(): lax.ppermute(value, axis, [(i, i ^ 1 << distance) for i in range(lax.axis...  87.2 us
    ppermute x8, waiting for transfers between devices, partner(): lax.ppermute(value, axis, [(i, i ^ 1 << distance) for i in range(lax.axis...  37.9 us
  transfers between devices with their start and end apart: 9, of which 6 were waited for; matrix products, arithmetic and copies ran while one was open for 1% of the time, Pallas kernels for 0%

commit v1 on v0

v1 whole, which is shorter than its diff:
```python
import jax
import jax.numpy as jnp
from jax import lax
from jax.experimental import pallas as pl
from jax.experimental.pallas import tpu as pltpu
from jax.sharding import PartitionSpec as P

HD = 128
GROUP = 2
N = 8
MESH = pl.DeviceIdType.MESH
F32 = jnp.float32
BF16 = jnp.bfloat16


def contract(a, b, dims):
    return lax.dot_general(a, b, ((dims[:1], dims[1:]), ((), ())), preferred_element_type=F32)


def heads_to_rows(x):
    return jnp.concatenate([x[:, h * HD : (h + 1) * HD] for h in range(x.shape[1] // HD)], axis=0)


def kernel(
    alive_ref, pos_ref, q_hbm, k_hbm, v_hbm, h_hbm, g_hbm,
    dq_hbm, dk_hbm, gw_ref,
    q_buf, k_buf, v_buf, g_buf, h_buf, mask_buf, p_buf, gv_buf, dq_buf, dk_buf,
    gv_send, gv_recv, gv_chunk, part, r_send, r_recv, s2_send, s2_recv, s3_send, s3_recv,
    in_sem, h_sem, out_sem, gs_sem, gr_sem, rs_sem, rr_sem, s2s_sem, s2r_sem, s3s_sem, s3r_sem,
):
    rows, length, _ = q_buf.shape
    cols = h_buf.shape[-1]
    heads = q_buf.shape[-1] // HD
    width = heads * length
    factor = HD**-0.5

    dp = lax.axis_index("dp")
    tensor = lax.axis_index("tensor")
    core = lax.rem(tensor, 2)
    x_hi = lax.rem(dp, 2)
    y = lax.rem(dp // 2, N)
    z = dp // (2 * N)
    stride = 2 * N - (2 * N - 2) * core
    ring = z * (1 - core) + y * core
    stride2 = 2 + (2 * N - 2) * core
    ring2 = y * (1 - core) + z * core

    def on_ring(d):
        return dp + (lax.rem(ring + d + N, N) - ring) * stride

    def on_ring2(d):
        return dp + (lax.rem(ring2 + d, N) - ring2) * stride2

    peers = [(dp, lax.rem(tensor + d, N)) for d in range(1, N)]
    peers += [(on_ring(1), tensor), (on_ring(-1), tensor)]
    peers += [(on_ring2(d), tensor) for d in range(1, N)]
    far = dp + 1 - 2 * x_hi
    peers += [(far, tensor), (far, tensor + 1 - 2 * core)]

    barrier = pltpu.get_barrier_semaphore()
    for peer in peers:
        pl.semaphore_signal(barrier, inc=1, device_id=peer, device_id_type=MESH)

    def load_row(r):
        return (
            pltpu.make_async_copy(q_hbm.at[r], q_buf.at[r], in_sem.at[r]),
            pltpu.make_async_copy(g_hbm.at[r], g_buf.at[r], in_sem.at[rows + r]),
        )

    load_k = pltpu.make_async_copy(k_hbm, k_buf, in_sem.at[2 * rows])
    load_v = pltpu.make_async_copy(v_hbm, v_buf, in_sem.at[2 * rows + 1])
    load_h = pltpu.make_async_copy(h_hbm, h_buf.at[core], in_sem.at[2 * rows + 2])
    load_k.start()
    for r in range(rows):
        for copy in load_row(r):
            copy.start()
    load_v.start()
    load_h.start()

    k_index = lax.broadcasted_iota(jnp.int32, (length, width), 0)
    lane = lax.broadcasted_iota(jnp.int32, (length, width), 1)
    q_index = lane
    for h in range(1, heads):
        q_index = jnp.where(lane >= h * length, lane - h * length, q_index)
    mask_buf[...] = jnp.where(k_index < q_index, k_index, jnp.where(k_index == q_index, length, -1))

    def masked_grad(r):
        alive = alive_ref[dp * (rows // GROUP) + r // GROUP].astype(F32).astype(BF16)
        return heads_to_rows(g_buf[r] * alive)

    load_k.wait()

    def forward(r, carry):
        for copy in load_row(r):
            copy.wait()
        queries = heads_to_rows(q_buf[r])
        grads = masked_grad(r)
        scores = contract(k_buf[r], queries, (1, 1)) * factor
        scores = jnp.where(mask_buf[...] >= -pos_ref[r, 0], scores, F32(-1e30))
        expo = jnp.exp(scores - jnp.max(scores, axis=0, keepdims=True))
        probs = expo * (1.0 / jnp.sum(expo, axis=0, keepdims=True))
        p_buf[r] = probs
        at = pl.ds(pl.multiple_of(r * length, length), length)
        gv_buf[at, :] = contract(probs.astype(BF16), grads, (1, 0))
        return carry

    lax.fori_loop(0, rows, forward, 0)

    value_grad = gv_buf[...].T
    tokens = value_grad.shape[1]
    value_grad = value_grad.reshape(HD // 16, 2, 8, tokens)
    for c in range(2):
        gv_send[c] = value_grad[:, c].reshape(HD // 2, tokens).astype(BF16)

    pl.semaphore_wait(barrier, len(peers))

    def give(d):
        to = lax.rem(tensor + d, N)
        return pltpu.make_async_remote_copy(
            src_ref=gv_send.at[lax.rem(to, 2)], dst_ref=gv_recv.at[tensor],
            send_sem=gs_sem.at[d], recv_sem=gr_sem.at[tensor],
            device_id=(dp, to), device_id_type=MESH,
        )

    def take(d):
        of = lax.rem(tensor + d, N)
        return pltpu.make_async_remote_copy(
            src_ref=gv_send.at[0], dst_ref=gv_recv.at[of],
            send_sem=gs_sem.at[d], recv_sem=gr_sem.at[of],
            device_id=(dp, of), device_id_type=MESH,
        )

    for d in (4, 3, 5, 2, 6, 1, 7):
        give(d).start()
    swap_h = pltpu.make_async_remote_copy(
        src_ref=h_hbm, dst_ref=h_buf.at[core], send_sem=h_sem.at[0], recv_sem=h_sem.at[1],
        device_id=(dp, tensor + 1 - 2 * core), device_id_type=MESH,
    )
    swap_h.start()
    gv_recv[tensor] = gv_send[core]
    load_v.wait()

    def store_row(r):
        return pltpu.make_async_copy(dq_buf.at[r], dq_hbm.at[r], out_sem.at[r])

    def backward(r, carry):
        queries = heads_to_rows(q_buf[r])
        grads = masked_grad(r)
        probs = p_buf[r]
        dprobs = contract(v_buf[r], grads, (1, 1))
        delta = jnp.sum(probs.astype(BF16).astype(F32) * dprobs, axis=0, keepdims=True)
        dscores = (probs * (dprobs - delta)).astype(BF16)
        dk_buf[r] = (contract(dscores, queries, (1, 0)) * factor).astype(BF16)
        dq = (contract(dscores, k_buf[r], (0, 0)) * factor).astype(BF16)
        for h in range(heads):
            dq_buf[r, :, h * HD : (h + 1) * HD] = dq[h * length : (h + 1) * length]
        store_row(r).start()
        return carry

    lax.fori_loop(0, rows, backward, 0)
    store_dk = pltpu.make_async_copy(dk_buf, dk_hbm, out_sem.at[rows])
    store_dk.start()

    for d in (1, 7, 2, 6, 3, 5, 4):
        take(d).wait_recv()

    @pl.when(core == 0)
    def _():
        gv_chunk[...] = gv_recv[...]

    @pl.when(core == 1)
    def _():
        for t in range(N):
            gv_chunk[t] = jnp.concatenate(
                [gv_recv[h].astype(F32)[8 * t : 8 * t + 8] for h in range(N)], axis=0
            ).astype(BF16)

    load_h.wait()
    swap_h.wait_recv()

    def product(d, k):
        at = lax.rem(ring + d + N, N)
        hidden = h_buf[k].reshape(tokens, cols)
        return contract(gv_chunk[at], hidden, (1, 0))

    def hop(way, k, j):
        return pltpu.make_async_remote_copy(
            src_ref=r_send.at[way, k, j], dst_ref=r_recv.at[way, k, j],
            send_sem=rs_sem.at[way, k, j], recv_sem=rr_sem.at[way, k, j],
            device_id=(on_ring(1 - 2 * way), tensor), device_id_type=MESH,
        )

    def ahead(way, j):
        return (4 - j) * (1 - 2 * way)

    for way, k, j in ((0, 0, 0), (1, 1, 0), (0, 1, 1), (1, 0, 1)):
        r_send[way, k, j] = product(ahead(way, j), k).astype(BF16)
        hop(way, k, j).start()
    for j in range(1, 4):
        for first in (True, False):
            pair = ((0, 0), (1, 1)) if first else ((0, 1), (1, 0))
            step = j if first else j + 1
            if step == 4:
                continue
            for way, k in pair:
                part[way] = product(ahead(way, step), k)
            for way, k in pair:
                hop(way, k, step - 1).wait_recv()
                r_send[way, k, step] = (part[way] + r_recv[way, k, step - 1].astype(F32)).astype(BF16)
                hop(way, k, step).start()
    for k in range(2):
        part[k] = product(0, k)
    sums = []
    for k in range(2):
        total = part[k]
        for way in range(2):
            hop(way, k, 3).wait_recv()
            total = total + r_recv[way, k, 3].astype(F32)
        sums.append(total.reshape(N, 8, cols))
    s2_send[...] = jnp.concatenate(sums, axis=1).astype(BF16)

    def cross(d):
        to = lax.rem(ring2 + d, N)
        return pltpu.make_async_remote_copy(
            src_ref=s2_send.at[to], dst_ref=s2_recv.at[ring2],
            send_sem=s2s_sem.at[d], recv_sem=s2r_sem.at[ring2],
            device_id=(on_ring2(d), tensor), device_id_type=MESH,
        )

    def cross_in(d):
        of = lax.rem(ring2 + d, N)
        return pltpu.make_async_remote_copy(
            src_ref=s2_send.at[of], dst_ref=s2_recv.at[of],
            send_sem=s2s_sem.at[d], recv_sem=s2r_sem.at[of],
            device_id=(on_ring2(d), tensor), device_id_type=MESH,
        )

    for d in (4, 3, 5, 2, 6, 1, 7):
        cross(d).start()
    total = s2_send[ring2].astype(F32)
    for d in (1, 7, 2, 6, 3, 5, 4):
        cross_in(d).wait_recv()
        total = total + s2_recv[lax.rem(ring2 + d, N)].astype(F32)
    for k in range(2):
        s3_send[k] = total[8 * k : 8 * k + 8]

    def finish(k):
        return pltpu.make_async_remote_copy(
            src_ref=s3_send.at[k], dst_ref=s3_recv.at[x_hi],
            send_sem=s3s_sem.at[k], recv_sem=s3r_sem.at[x_hi],
            device_id=(dp - x_hi + core, tensor - core + k), device_id_type=MESH,
        )

    def finish_in(of):
        return pltpu.make_async_remote_copy(
            src_ref=s3_send.at[0], dst_ref=s3_recv.at[of],
            send_sem=s3s_sem.at[0], recv_sem=s3r_sem.at[of],
            device_id=(far, tensor), device_id_type=MESH,
        )

    home = x_hi == core

    @pl.when(home)
    def _():
        finish(1 - core).start()
        finish_in(1 - x_hi).wait_recv()
        gw_ref[...] = s3_send[core] + s3_recv[1 - x_hi]
        finish(1 - core).wait_send()

    @pl.when(jnp.logical_not(home))
    def _():
        for k in range(2):
            finish(k).start()
        for of in range(2):
            finish_in(of).wait_recv()
        gw_ref[...] = s3_recv[0] + s3_recv[1]
        for k in range(2):
            finish(k).wait_send()

    for d in range(1, N):
        give(d).wait_send()
        cross(d).wait_send()
    swap_h.wait_send()
    for way in range(2):
        for k in range(2):
            for j in range(0 if way == k else 1, 4):
                hop(way, k, j).wait_send()
    for r in range(rows):
        store_row(r).wait()
    store_dk.wait()


def local(queries, keys, values, hidden, grad_out, group_alive, positions):
    rows, length, model = queries.shape
    cols = hidden.shape[-1]
    heads = model // HD
    width = heads * length
    tokens = rows * length
    half = HD // 2
    anywhere = pl.BlockSpec(memory_space=pl.ANY)
    scalar = pl.BlockSpec(memory_space=pltpu.SMEM)
    dma = pltpu.SemaphoreType.DMA
    return pl.pallas_call(
        kernel,
        out_shape=(
            jax.ShapeDtypeStruct(queries.shape, BF16),
            jax.ShapeDtypeStruct(keys.shape, BF16),
            jax.ShapeDtypeStruct((8, cols), F32),
        ),
        in_specs=[scalar, scalar] + [anywhere] * 5,
        out_specs=(anywhere, anywhere, pl.BlockSpec(memory_space=pltpu.VMEM)),
        scratch_shapes=[
            pltpu.VMEM(queries.shape, BF16),
            pltpu.VMEM(keys.shape, BF16),
            pltpu.VMEM(keys.shape, BF16),
            pltpu.VMEM(queries.shape, BF16),
            pltpu.VMEM((2,) + hidden.shape, BF16),
            pltpu.VMEM((length, width), jnp.int32),
            pltpu.VMEM((rows, length, width), F32),
            pltpu.VMEM((tokens, HD), F32),
            pltpu.VMEM(queries.shape, BF16),
            pltpu.VMEM(keys.shape, BF16),
            pltpu.VMEM((2, half, tokens), BF16),
            pltpu.VMEM((N, half, tokens), BF16),
            pltpu.VMEM((N, half, tokens), BF16),
            pltpu.VMEM((2, half, cols), F32),
            pltpu.VMEM((2, 2, 4, half, cols), BF16),
            pltpu.VMEM((2, 2, 4, half, cols), BF16),
            pltpu.VMEM((N, 16, cols), BF16),
            pltpu.VMEM((N, 16, cols), BF16),
            pltpu.VMEM((2, 8, cols), F32),
            pltpu.VMEM((2, 8, cols), F32),
            dma((2 * rows + 3,)),
            dma((2,)),
            dma((rows + 1,)),
            dma((N,)),
            dma((N,)),
            dma((2, 2, 4)),
            dma((2, 2, 4)),
            dma((N,)),
            dma((N,)),
            dma((2,)),
            dma((2,)),
        ],
        compiler_params=pltpu.CompilerParams(
            collective_id=0, has_side_effects=True, vmem_limit_bytes=40 * 1024 * 1024
        ),
        cost_estimate=pl.CostEstimate(
            flops=10 * width * length * HD * rows + 2 * tokens * 1024 * cols,
            bytes_accessed=4000000,
            transcendentals=rows * width * length,
        ),
    )(group_alive, positions, queries, keys, values, hidden, grad_out)


def solution(mesh):
    return jax.shard_map(
        local,
        mesh=mesh,
        in_specs=(
            P("dp", None, "tensor"),
            P("dp", None, "tensor"),
            P("dp", None, "tensor"),
            P("dp", None, "tensor"),
            P("dp", None, "tensor"),
            P(),
            P("dp", None),
        ),
        out_specs=(P("dp", None, "tensor"), P("dp", None, "tensor"), P("dp", "tensor")),
        check_vma=False,
    )
```

time: 1800 us -> 70 us (0.04)
  the two profiles are of different devices: /device:TPU:8 before, /device:TPU:1 now
where the time goes in v1:
time: 70 us; the launch traced here: 69.5 us
  Pallas kernels  60.3 us (86%)
  local copies, waits for them, and re-layouts  8.56 us (12%)
    pallas_call x1, Pallas kernels, local(): pl.pallas_call(kernel, out_shape=(jax.ShapeDtypeStruct(queries.shape, BF1...  60.3 us
    unnamed x17, local copies, waits for them, and re-layouts  8.56 us

profile of v1, /device:TPU:1, one launch (start us, length us, event | category | flops | bytes accessed | tf_op | source)
XLA Modules:
  0.0 69.5 jit_solution(7679593031729858951)
XLA Ops:
  0.6 0.0 copy-start
  0.6 1.1 %copy-done = bf16[4,96,1024]{2,1,0:T(8,128)(2,1)S(1)} copy-done((bf16[4,96,1024]{2,1,0:T(8,128)(2,1)S(1)}, bf16[4,96,1024]{2,1,0:T(8,128)(2,1)}, u32[]{:S(2)}) %copy-start) | copy-done | bytes 786456
  1.8 0.0 copy-start.1
  1.8 1.1 %copy-done.1 = bf16[4,96,1024]{2,1,0:T(8,128)(2,1)S(1)} copy-done((bf16[4,96,1024]{2,1,0:T(8,128)(2,1)S(1)}, bf16[4,96,1024]{2,1,0:T(8,128)(2,1)}, u32[]{:S(2)}) %copy-start.1) | copy-done | bytes 786456
  2.9 0.0 copy-start.2
  2.9 1.0 %copy-done.2 = bf16[4,96,640]{2,1,0:T(8,128)(2,1)S(1)} copy-done((bf16[4,96,640]{2,1,0:T(8,128)(2,1)S(1)}, bf16[4,96,640]{2,1,0:T(8,128)(2,1)}, u32[]{:S(2)}) %copy-start.2) | copy-done | bytes 491544
  3.9 0.0 copy-start.3
  3.9 0.9 %copy-done.3 = bf16[4,96,128]{2,1,0:T(8,128)(2,1)S(1)} copy-done((bf16[4,96,128]{2,1,0:T(8,128)(2,1)S(1)}, bf16[4,96,128]{2,1,0:T(8,128)(2,1)}, u32[]{:S(2)}) %copy-start.3) | copy-done | bytes 98328
  4.8 0.0 copy-start.4
  4.8 0.9 %copy-done.4 = bf16[4,96,128]{2,1,0:T(8,128)(2,1)S(1)} copy-done((bf16[4,96,128]{2,1,0:T(8,128)(2,1)S(1)}, bf16[4,96,128]{2,1,0:T(8,128)(2,1)}, u32[]{:S(2)}) %copy-start.4) | copy-done | bytes 98328
  5.7 0.0 copy-start.5
  5.7 0.7 copy-done.5
  6.4 0.0 copy-start.6
  6.4 0.7 copy-done.6
  7.1 60.3 %shard_map.94 = (bf16[4,96,1024]{2,1,0:T(8,128)(2,1)S(1)}, bf16[4,96,128]{2,1,0:T(8,128)(2,1)S(1)}, f32[8,640]{1,0:T(8,128)S(1)}) custom-call(s32[256]{0:T(256)S(1)} %copy-done.6, s32[4,96]{1,0:T(4,128)S(1)} %copy-done.5, bf16[4,96,1024]{2,1,0:T(8,128)(2,1)S(1)} %copy-done, bf16[4,96,128]{2,1,0:T(8,128)(2,1)S(1)} %copy-done.3, ...), custom_call_target="tpu_custom_call" | custom-call | flops 880803840 | bytes 4000000 | tf_op jit(solution)/shard_map/pallas_call | solution.py:303
  67.4 0.9 %copy.13 = bf16[4,96,1024]{2,1,0:T(8,128)(2,1)} copy(bf16[4,96,1024]{2,1,0:T(8,128)(2,1)S(1)} %get-tuple-element.6) | data formatting | bytes 1572864
  68.3 0.6 copy.14
  68.9 0.6 copy.15
Async XLA Ops:
  0.6 1.1 %copy-start = (bf16[4,96,1024]{2,1,0:T(8,128)(2,1)S(1)}, bf16[4,96,1024]{2,1,0:T(8,128)(2,1)}, u32[]{:S(2)}) copy-start(bf16[4,96,1024]{2,1,0:T(8,128)(2,1)} %q_hbm.1) | copy-start | bytes 2359300
  1.8 1.1 %copy-start.1 = (bf16[4,96,1024]{2,1,0:T(8,128)(2,1)S(1)}, bf16[4,96,1024]{2,1,0:T(8,128)(2,1)}, u32[]{:S(2)}) copy-start(bf16[4,96,1024]{2,1,0:T(8,128)(2,1)} %g_hbm.1) | copy-start | bytes 2359300
  2.9 1.0 %copy-start.2 = (bf16[4,96,640]{2,1,0:T(8,128)(2,1)S(1)}, bf16[4,96,640]{2,1,0:T(8,128)(2,1)}, u32[]{:S(2)}) copy-start(bf16[4,96,640]{2,1,0:T(8,128)(2,1)} %h_hbm.1) | copy-start | bytes 1474564
  3.9 0.9 %copy-start.3 = (bf16[4,96,128]{2,1,0:T(8,128)(2,1)S(1)}, bf16[4,96,128]{2,1,0:T(8,128)(2,1)}, u32[]{:S(2)}) copy-start(bf16[4,96,128]{2,1,0:T(8,128)(2,1)} %k_hbm.1) | copy-start | bytes 294916
  4.8 0.9 %copy-start.4 = (bf16[4,96,128]{2,1,0:T(8,128)(2,1)S(1)}, bf16[4,96,128]{2,1,0:T(8,128)(2,1)}, u32[]{:S(2)}) copy-start(bf16[4,96,128]{2,1,0:T(8,128)(2,1)} %v_hbm.1) | copy-start | bytes 294916
  5.7 0.7 copy-start.5
  6.4 0.7 copy-start.6

commit v2 on v1

v2 whole, which is shorter than its diff:
```python
import jax
import jax.numpy as jnp
from jax import lax
from jax.experimental import pallas as pl
from jax.experimental.pallas import tpu as pltpu
from jax.sharding import PartitionSpec as P

HD = 128
GROUP = 2
N = 8
MESH = pl.DeviceIdType.MESH
F32 = jnp.float32
BF16 = jnp.bfloat16


def contract(a, b, dims):
    return lax.dot_general(a, b, ((dims[:1], dims[1:]), ((), ())), preferred_element_type=F32)


def heads_to_rows(x):
    return jnp.concatenate([x[:, h * HD : (h + 1) * HD] for h in range(x.shape[1] // HD)], axis=0)


def kernel(
    q_hbm, k_hbm, v_hbm, h_hbm, g_hbm, alive_hbm, pos_hbm,
    dq_ref, dk_ref, gw_ref,
    q_buf, k_buf, v_buf, g_buf, h_buf, mask_buf, p_buf, gv_buf, alive_ref, pos_ref,
    gv_half, gv_whole, gv_recv, gv_chunk, part, r_send, r_recv, s2_send, s2_recv, s3_send, s3_recv,
    in_sem, h_sem, gs_sem, gr_sem, ws_sem, wr_sem, rs_sem, rr_sem, s2s_sem, s2r_sem, s3s_sem, s3r_sem,
):
    rows, length, _ = q_buf.shape
    cols = h_buf.shape[-1]
    heads = q_buf.shape[-1] // HD
    width = heads * length
    tokens = rows * length
    factor = HD**-0.5
    piece = HD // 4

    dp = lax.axis_index("dp")
    tensor = lax.axis_index("tensor")
    core = lax.rem(tensor, 2)
    x_hi = lax.rem(dp, 2)
    y = lax.rem(dp // 2, N)
    z = dp // (2 * N)
    stride = 2 * N - (2 * N - 2) * core
    ring = z * (1 - core) + y * core
    stride2 = 2 + (2 * N - 2) * core
    ring2 = y * (1 - core) + z * core

    def on_ring(d):
        return dp + (lax.rem(ring + d + N, N) - ring) * stride

    def at_ring2(place):
        return dp + (place - ring2) * stride2

    load_scalars = (
        pltpu.make_async_copy(alive_hbm, alive_ref, in_sem.at[2 * rows + 3]),
        pltpu.make_async_copy(pos_hbm, pos_ref, in_sem.at[2 * rows + 4]),
    )

    def load_row(r):
        return (
            pltpu.make_async_copy(q_hbm.at[r], q_buf.at[r], in_sem.at[r]),
            pltpu.make_async_copy(g_hbm.at[r], g_buf.at[r], in_sem.at[rows + r]),
        )

    load_k = pltpu.make_async_copy(k_hbm, k_buf, in_sem.at[2 * rows])
    load_v = pltpu.make_async_copy(v_hbm, v_buf, in_sem.at[2 * rows + 1])
    load_h = pltpu.make_async_copy(h_hbm, h_buf.at[core], in_sem.at[2 * rows + 2])
    for copy in load_scalars:
        copy.start()
    load_k.start()
    for r in range(rows):
        for copy in load_row(r):
            copy.start()
    load_v.start()
    load_h.start()

    far = dp + 1 - 2 * x_hi
    peers = [(far, tensor), (far, tensor + 1 - 2 * core)]
    peers += [(at_ring2(lax.rem(ring2 + d, N)), tensor) for d in range(1, N)]
    peers += [(dp, lax.rem(tensor + d, N)) for d in range(1, N)]
    peers += [(on_ring(1), tensor), (on_ring(-1), tensor)]
    barrier = pltpu.get_barrier_semaphore()
    for peer in peers:
        pl.semaphore_signal(barrier, inc=1, device_id=peer, device_id_type=MESH)

    k_index = lax.broadcasted_iota(jnp.int32, (length, width), 0)
    lane = lax.broadcasted_iota(jnp.int32, (length, width), 1)
    q_index = lane
    for h in range(1, heads):
        q_index = jnp.where(lane >= h * length, lane - h * length, q_index)
    mask_buf[...] = jnp.where(k_index < q_index, k_index, jnp.where(k_index == q_index, length, -1))

    def masked_grad(r):
        alive = alive_ref[dp * (rows // GROUP) + r // GROUP].astype(F32).astype(BF16)
        return heads_to_rows(g_buf[r] * alive)

    for copy in load_scalars:
        copy.wait()
    load_k.wait()

    def forward(r, carry):
        for copy in load_row(r):
            copy.wait()
        queries = heads_to_rows(q_buf[r])
        grads = masked_grad(r)
        scores = contract(k_buf[r], queries, (1, 1)) * factor
        scores = jnp.where(mask_buf[...] >= -pos_ref[r, 0], scores, F32(-1e30))
        expo = jnp.exp(scores - jnp.max(scores, axis=0, keepdims=True))
        probs = expo * (1.0 / jnp.sum(expo, axis=0, keepdims=True))
        p_buf[r] = probs
        at = pl.ds(pl.multiple_of(r * length, length), length)
        gv_buf[at, :] = contract(probs.astype(BF16), grads, (1, 0))
        return carry

    lax.fori_loop(0, rows, forward, 0)

    value_grad = gv_buf[...].T.reshape(HD // 16, 2, 8, tokens)
    for s in range(2):
        gv_half[s] = value_grad[4 * s : 4 * s + 4, 0].reshape(piece, tokens).astype(BF16)
    gv_whole[...] = value_grad[:, 1].reshape(2 * piece, tokens).astype(BF16)

    pl.semaphore_wait(barrier, len(peers))

    def give_half(s, chip):
        return pltpu.make_async_remote_copy(
            src_ref=gv_half.at[s], dst_ref=gv_chunk.at[s, tensor],
            send_sem=gs_sem.at[s, chip], recv_sem=gr_sem.at[s, tensor],
            device_id=(dp, 2 * chip), device_id_type=MESH,
        )

    def take_half(s, of):
        return pltpu.make_async_remote_copy(
            src_ref=gv_half.at[s], dst_ref=gv_chunk.at[s, of],
            send_sem=gs_sem.at[s, 0], recv_sem=gr_sem.at[s, of],
            device_id=(dp, of), device_id_type=MESH,
        )

    def give_whole(chip):
        return pltpu.make_async_remote_copy(
            src_ref=gv_whole, dst_ref=gv_recv.at[tensor],
            send_sem=ws_sem.at[chip], recv_sem=wr_sem.at[tensor],
            device_id=(dp, 2 * chip + 1), device_id_type=MESH,
        )

    def take_whole(of):
        return pltpu.make_async_remote_copy(
            src_ref=gv_whole, dst_ref=gv_recv.at[of],
            send_sem=ws_sem.at[0], recv_sem=wr_sem.at[of],
            device_id=(dp, of), device_id_type=MESH,
        )

    chips = N // 2
    own = tensor // 2
    away = [lax.rem(own + d, chips) for d in (2, 1, 3)]
    for s in range(2):
        for chip in away:
            give_half(s, chip).start()

        @pl.when(core == s)
        def _():
            for chip in away:
                give_whole(chip).start()

        @pl.when(core == 1)
        def _():
            give_half(s, own).start()

    @pl.when(core == 0)
    def _():
        give_whole(own).start()
        for s in range(2):
            gv_chunk[s, tensor] = gv_half[s]

    @pl.when(core == 1)
    def _():
        gv_recv[tensor] = gv_whole[...]

    swap_h = pltpu.make_async_remote_copy(
        src_ref=h_hbm, dst_ref=h_buf.at[core], send_sem=h_sem.at[0], recv_sem=h_sem.at[1],
        device_id=(dp, tensor + 1 - 2 * core), device_id_type=MESH,
    )
    swap_h.start()
    load_v.wait()

    def backward(r, carry):
        queries = heads_to_rows(q_buf[r])
        grads = masked_grad(r)
        probs = p_buf[r]
        dprobs = contract(v_buf[r], grads, (1, 1))
        delta = jnp.sum(probs.astype(BF16).astype(F32) * dprobs, axis=0, keepdims=True)
        dscores = (probs * (dprobs - delta)).astype(BF16)
        dk_ref[r] = (contract(dscores, queries, (1, 0)) * factor).astype(BF16)
        dq = (contract(dscores, k_buf[r], (0, 0)) * factor).astype(BF16)
        for h in range(heads):
            dq_ref[r, :, h * HD : (h + 1) * HD] = dq[h * length : (h + 1) * length]
        return carry

    lax.fori_loop(0, rows, backward, 0)
    load_h.wait()
    swap_h.wait_recv()

    def gathered(s):
        @pl.when(core == 0)
        def _():
            for d in range(1, N):
                take_half(s, lax.rem(tensor + d, N)).wait_recv()

        @pl.when(core == 1)
        def _():
            for chip in range(chips):
                of = 2 * chip + s

                @pl.when(of != tensor)
                def _():
                    take_whole(of).wait_recv()

            parts = [gv_recv[2 * chip + s].astype(F32) for chip in range(chips)]
            for t in range(N):
                gv_chunk[s, t] = jnp.concatenate([x[8 * t : 8 * t + 8] for x in parts], axis=0).astype(BF16)

    def products(s, offsets):
        left = jnp.concatenate([gv_chunk[s, lax.rem(ring + d + N, N)] for d in offsets], axis=0)
        for k in range(2):
            both = contract(left, h_buf[k].reshape(tokens, cols), (1, 0))
            for i in range(len(offsets)):
                part[s, i, k] = both[i * piece : (i + 1) * piece]

    def hop(way, s, j):
        return pltpu.make_async_remote_copy(
            src_ref=r_send.at[way, s, j], dst_ref=r_recv.at[way, s, j],
            send_sem=rs_sem.at[way, s, j], recv_sem=rr_sem.at[way, s, j],
            device_id=(on_ring(1 - 2 * way), tensor), device_id_type=MESH,
        )

    def first_sends(s):
        products(s, (4,))
        r_send[s, s, 0] = part[s, 0].astype(BF16)
        hop(s, s, 0).start()
        products(s, (3, -3))
        r_send[1 - s, s, 1] = part[s, 1 - s].astype(BF16)
        hop(1 - s, s, 1).start()

    def pass_on(way, s, j):
        hop(way, s, j - 1).wait_recv()
        r_send[way, s, j] = (part[s, way] + r_recv[way, s, j - 1].astype(F32)).astype(BF16)
        hop(way, s, j).start()

    def round_two(s):
        pass_on(s, s, 1)
        products(s, (2, -2))

    def round_three(s):
        for way in (1 - s, s):
            pass_on(way, s, 2)
        products(s, (1, -1))

    def round_four(s):
        for way in (1 - s, s):
            pass_on(way, s, 3)
        products(s, (0,))

    def place2(i):
        return i * (1 - core) + (2 * (i % 4) + i // 4) * core

    def cross(i):
        return pltpu.make_async_remote_copy(
            src_ref=s2_send.at[i], dst_ref=s2_recv.at[ring2],
            send_sem=s2s_sem.at[i], recv_sem=s2r_sem.at[ring2],
            device_id=(at_ring2(place2(i)), tensor), device_id_type=MESH,
        )

    def cross_in(of):
        return pltpu.make_async_remote_copy(
            src_ref=s2_send.at[0], dst_ref=s2_recv.at[of],
            send_sem=s2s_sem.at[0], recv_sem=s2r_sem.at[of],
            device_id=(at_ring2(of), tensor), device_id_type=MESH,
        )

    def if_away(i, act):
        @pl.when(place2(i) != ring2)
        def _():
            act(cross(i))

    def ring_end(s):
        total = part[s, 0]
        for way in (1 - s, s):
            hop(way, s, 3).wait_recv()
            total = total + r_recv[way, s, 3].astype(F32)
        total = total.reshape(2, 4, 8, cols)
        s2_send[4 * s : 4 * s + 4] = jnp.concatenate([total[0], total[1]], axis=1).astype(BF16)
        for i in range(4 * s, 4 * s + 4):
            if_away(i, lambda copy: copy.start())

    gathered(0)
    first_sends(0)
    round_two(0)
    gathered(1)
    first_sends(1)
    round_three(0)
    round_two(1)
    round_four(0)
    round_three(1)
    ring_end(0)
    round_four(1)
    ring_end(1)

    mine = ring2 * (1 - core) + (ring2 // 2 + 4 * lax.rem(ring2, 2)) * core
    total = s2_send[mine].astype(F32)
    for d in (1, 7, 2, 6, 3, 5, 4):
        of = lax.rem(ring2 + d, N)
        cross_in(of).wait_recv()
        total = total + s2_recv[of].astype(F32)
    for k in range(2):
        s3_send[k] = total[8 * k : 8 * k + 8]

    def finish(k):
        return pltpu.make_async_remote_copy(
            src_ref=s3_send.at[k], dst_ref=s3_recv.at[x_hi],
            send_sem=s3s_sem.at[k], recv_sem=s3r_sem.at[x_hi],
            device_id=(dp - x_hi + core, tensor - core + k), device_id_type=MESH,
        )

    def finish_in(of):
        return pltpu.make_async_remote_copy(
            src_ref=s3_send.at[0], dst_ref=s3_recv.at[of],
            send_sem=s3s_sem.at[0], recv_sem=s3r_sem.at[of],
            device_id=(far, tensor), device_id_type=MESH,
        )

    home = x_hi == core

    @pl.when(home)
    def _():
        finish(1 - core).start()

    @pl.when(jnp.logical_not(home))
    def _():
        for k in range(2):
            finish(k).start()

    for s in range(2):
        for chip in away:
            give_half(s, chip).wait_send()
        for way in range(2):
            for j in range(0 if way == s else 1, 4):
                hop(way, s, j).wait_send()
    for chip in away:
        give_whole(chip).wait_send()

    @pl.when(core == 0)
    def _():
        give_whole(own).wait_send()

    @pl.when(core == 1)
    def _():
        for s in range(2):
            give_half(s, own).wait_send()

    for i in range(N):
        if_away(i, lambda copy: copy.wait_send())
    swap_h.wait_send()

    @pl.when(home)
    def _():
        finish_in(1 - x_hi).wait_recv()
        gw_ref[...] = s3_send[core] + s3_recv[1 - x_hi]
        finish(1 - core).wait_send()

    @pl.when(jnp.logical_not(home))
    def _():
        for of in range(2):
            finish_in(of).wait_recv()
        gw_ref[...] = s3_recv[0] + s3_recv[1]
        for k in range(2):
            finish(k).wait_send()


def local(queries, keys, values, hidden, grad_out, group_alive, positions):
    rows, length, model = queries.shape
    cols = hidden.shape[-1]
    heads = model // HD
    width = heads * length
    tokens = rows * length
    piece = HD // 4
    anywhere = pl.BlockSpec(memory_space=pl.ANY)
    inside = pl.BlockSpec(memory_space=pltpu.VMEM)
    dma = pltpu.SemaphoreType.DMA
    inputs = (queries, keys, values, hidden, grad_out, group_alive, positions)
    return pl.pallas_call(
        kernel,
        out_shape=(
            pltpu.VMEM(queries.shape, BF16),
            pltpu.VMEM(keys.shape, BF16),
            pltpu.VMEM((8, cols), F32),
        ),
        in_specs=[anywhere] * 7,
        out_specs=(inside,) * 3,
        scratch_shapes=[
            pltpu.VMEM(queries.shape, BF16),
            pltpu.VMEM(keys.shape, BF16),
            pltpu.VMEM(keys.shape, BF16),
            pltpu.VMEM(queries.shape, BF16),
            pltpu.VMEM((2,) + hidden.shape, BF16),
            pltpu.VMEM((length, width), jnp.int32),
            pltpu.VMEM((rows, length, width), F32),
            pltpu.VMEM((tokens, HD), F32),
            pltpu.SMEM(group_alive.shape, jnp.int32),
            pltpu.SMEM(positions.shape, jnp.int32),
            pltpu.VMEM((2, piece, tokens), BF16),
            pltpu.VMEM((2 * piece, tokens), BF16),
            pltpu.VMEM((N, 2 * piece, tokens), BF16),
            pltpu.VMEM((2, N, piece, tokens), BF16),
            pltpu.VMEM((2, 2, 2, piece, cols), F32),
            pltpu.VMEM((2, 2, 4, 2, piece, cols), BF16),
            pltpu.VMEM((2, 2, 4, 2, piece, cols), BF16),
            pltpu.VMEM((N, 16, cols), BF16),
            pltpu.VMEM((N, 16, cols), BF16),
            pltpu.VMEM((2, 8, cols), F32),
            pltpu.VMEM((2, 8, cols), F32),
            dma((2 * rows + 5,)),
            dma((2,)),
            dma((2, N // 2)),
            dma((2, N)),
            dma((N // 2,)),
            dma((N,)),
            dma((2, 2, 4)),
            dma((2, 2, 4)),
            dma((N,)),
            dma((N,)),
            dma((2,)),
            dma((2,)),
        ],
        compiler_params=pltpu.CompilerParams(
            collective_id=0, has_side_effects=True, vmem_limit_bytes=40 * 1024 * 1024
        ),
        cost_estimate=pl.CostEstimate(
            flops=10 * width * length * HD * rows + 2 * tokens * 1024 * cols,
            bytes_accessed=4000000,
            transcendentals=rows * width * length,
        ),
    )(*(pltpu.with_memory_space_constraint(x, pltpu.HBM) for x in inputs))


def solution(mesh):
    return jax.shard_map(
        local,
        mesh=mesh,
        in_specs=(
            P("dp", None, "tensor"),
            P("dp", None, "tensor"),
            P("dp", None, "tensor"),
            P("dp", None, "tensor"),
            P("dp", None, "tensor"),
            P(),
            P("dp", None),
        ),
        out_specs=(P("dp", None, "tensor"), P("dp", None, "tensor"), P("dp", "tensor")),
        check_vma=False,
    )
```

time: 70 us -> 59.1 us (0.84)
  the two profiles are of different devices: /device:TPU:1 before, /device:TPU:99 now
where the time goes in v2:
time: 59.1 us; the launch traced here: 58.9 us
  Pallas kernels  56.2 us (95%)
  local copies, waits for them, and re-layouts  2.13 us (4%)
  between operations  0.64 us (1%)
    pallas_call x1, Pallas kernels, local(): pl.pallas_call(kernel, out_shape=(pltpu.VMEM(queries.shape, BF16), pltpu....  56.2 us
    unnamed x3, local copies, waits for them, and re-layouts  2.13 us

profile of v2, /device:TPU:99, one launch (start us, length us, event | category | flops | bytes accessed | tf_op | source)
XLA Modules:
  0.0 58.9 jit_solution(11259611733824101090)
XLA Ops:
  0.6 56.2 %shard_map.94 = (bf16[4,96,1024]{2,1,0:T(8,128)(2,1)S(1)}, bf16[4,96,128]{2,1,0:T(8,128)(2,1)S(1)}, f32[8,640]{1,0:T(8,128)S(1)}) custom-call(bf16[4,96,1024]{2,1,0:T(8,128)(2,1)} %q_hbm.1, bf16[4,96,128]{2,1,0:T(8,128)(2,1)} %k_hbm.1, bf16[4,96,128]{2,1,0:T(8,128)(2,1)} %v_hbm.1, bf16[4,96,640]{2,1,0:T(8,128)(2,1)} %h_hbm.1, bf16[4,96,1024]{2,1,0:T(8,128)(2,1)} %g_hbm.1, ...), custom_call_target="tpu_custom_call" | custom-call | flops 880803840 | bytes 4000000 | tf_op jit(solution)/shard_map/pallas_call | solution.py:391
  56.8 0.9 %copy.13 = bf16[4,96,1024]{2,1,0:T(8,128)(2,1)} copy(bf16[4,96,1024]{2,1,0:T(8,128)(2,1)S(1)} %get-tuple-element.3) | data formatting | bytes 1572864
  57.7 0.6 %copy.15 = f32[8,640]{1,0:T(8,128)} copy(f32[8,640]{1,0:T(8,128)S(1)} %get-tuple-element.5) | data formatting | bytes 40960
  58.3 0.6 %copy.14 = bf16[4,96,128]{2,1,0:T(8,128)(2,1)} copy(bf16[4,96,128]{2,1,0:T(8,128)(2,1)S(1)} %get-tuple-element.4) | data formatting | bytes 196608

commit v3 on v2

--- a/solution.py
+++ b/solution.py
@@ -53,6 +53,15 @@
     def at_ring2(place):
         return dp + (place - ring2) * stride2
 
+    far = dp + 1 - 2 * x_hi
+    peers = [(far, tensor), (far, tensor + 1 - 2 * core)]
+    peers += [(at_ring2(lax.rem(ring2 + d, N)), tensor) for d in range(1, N)]
+    peers += [(dp, lax.rem(tensor + d, N)) for d in range(1, N)]
+    peers += [(on_ring(d), tensor) for d in (2, -2, 1, -1)]
+    barrier = pltpu.get_barrier_semaphore()
+    for peer in peers:
+        pl.semaphore_signal(barrier, inc=1, device_id=peer, device_id_type=MESH)
+
     load_scalars = (
         pltpu.make_async_copy(alive_hbm, alive_ref, in_sem.at[2 * rows + 3]),
         pltpu.make_async_copy(pos_hbm, pos_ref, in_sem.at[2 * rows + 4]),
@@ -75,15 +84,6 @@
             copy.start()
     load_v.start()
     load_h.start()
-
-    far = dp + 1 - 2 * x_hi
-    peers = [(far, tensor), (far, tensor + 1 - 2 * core)]
-    peers += [(at_ring2(lax.rem(ring2 + d, N)), tensor) for d in range(1, N)]
-    peers += [(dp, lax.rem(tensor + d, N)) for d in range(1, N)]
-    peers += [(on_ring(1), tensor), (on_ring(-1), tensor)]
-    barrier = pltpu.get_barrier_semaphore()
-    for peer in peers:
-        pl.semaphore_signal(barrier, inc=1, device_id=peer, device_id_type=MESH)
 
     k_index = lax.broadcasted_iota(jnp.int32, (length, width), 0)
     lane = lax.broadcasted_iota(jnp.int32, (length, width), 1)
@@ -231,32 +231,32 @@
         return pltpu.make_async_remote_copy(
             src_ref=r_send.at[way, s, j], dst_ref=r_recv.at[way, s, j],
             send_sem=rs_sem.at[way, s, j], recv_sem=rr_sem.at[way, s, j],
-            device_id=(on_ring(1 - 2 * way), tensor), device_id_type=MESH,
+            device_id=(on_ring((1 if j else 2) * (1 - 2 * way)), tensor), device_id_type=MESH,
         )
 
     def first_sends(s):
-        products(s, (4,))
-        r_send[s, s, 0] = part[s, 0].astype(BF16)
+        products(s, (3, -3, 4))
+        r_send[s, s, 0] = part[s, 2].astype(BF16)
         hop(s, s, 0).start()
-        products(s, (3, -3))
-        r_send[1 - s, s, 1] = part[s, 1 - s].astype(BF16)
-        hop(1 - s, s, 1).start()
+        for way in (s, 1 - s):
+            r_send[way, s, 1] = part[s, way].astype(BF16)
+            hop(way, s, 1).start()
+        products(s, (2, -2))
 
     def pass_on(way, s, j):
-        hop(way, s, j - 1).wait_recv()
-        r_send[way, s, j] = (part[s, way] + r_recv[way, s, j - 1].astype(F32)).astype(BF16)
+        total = part[s, way]
+        for k in ((0, 1) if j == 2 and way == s else (j - 1,)):
+            hop(way, s, k).wait_recv()
+            total = total + r_recv[way, s, k].astype(F32)
+        r_send[way, s, j] = total.astype(BF16)
         hop(way, s, j).start()
 
-    def round_two(s):
-        pass_on(s, s, 1)
-        products(s, (2, -2))
-
-    def round_three(s):
+    def second_sends(s):
         for way in (1 - s, s):
             pass_on(way, s, 2)
         products(s, (1, -1))
 
-    def round_four(s):
+    def last_sends(s):
         for way in (1 - s, s):
             pass_on(way, s, 3)
         products(s, (0,))
@@ -295,16 +295,34 @@
 
     gathered(0)
     first_sends(0)
-    round_two(0)
+    second_sends(0)
     gathered(1)
     first_sends(1)
-    round_three(0)
-    round_two(1)
-    round_four(0)
-    round_three(1)
+    last_sends(0)
+    second_sends(1)
+    last_sends(1)
     ring_end(0)
-    round_four(1)
     ring_end(1)
+
+    for s in range(2):
+        for chip in away:
+            give_half(s, chip).wait_send()
+        for way in range(2):
+            for j in range(0 if way == s else 1, 4):
+                hop(way, s, j).wait_send()
+    for chip in away:
+        give_whole(chip).wait_send()
+
+    @pl.when(core == 0)
+    def _():
+        give_whole(own).wait_send()
+
+    @pl.when(core == 1)
+    def _():
+        for s in range(2):
+            give_half(s, own).wait_send()
+
+    swap_h.wait_send()
 
     mine = ring2 * (1 - core) + (ring2 // 2 + 4 * lax.rem(ring2, 2)) * core
     total = s2_send[mine].astype(F32)
@@ -340,27 +358,8 @@
         for k in range(2):
             finish(k).start()
 
-    for s in range(2):
-        for chip in away:
-            give_half(s, chip).wait_send()
-        for way in range(2):
-            for j in range(0 if way == s else 1, 4):
-                hop(way, s, j).wait_send()
-    for chip in away:
-        give_whole(chip).wait_send()
-
-    @pl.when(core == 0)
-    def _():
-        give_whole(own).wait_send()
-
-    @pl.when(core == 1)
-    def _():
-        for s in range(2):
-            give_half(s, own).wait_send()
-
     for i in range(N):
         if_away(i, lambda copy: copy.wait_send())
-    swap_h.wait_send()
 
     @pl.when(home)
     def _():
@@ -412,7 +411,7 @@
             pltpu.VMEM((2 * piece, tokens), BF16),
             pltpu.VMEM((N, 2 * piece, tokens), BF16),
             pltpu.VMEM((2, N, piece, tokens), BF16),
-            pltpu.VMEM((2, 2, 2, piece, cols), F32),
+            pltpu.VMEM((2, 3, 2, piece, cols), F32),
             pltpu.VMEM((2, 2, 4, 2, piece, cols), BF16),
             pltpu.VMEM((2, 2, 4, 2, piece, cols), BF16),
             pltpu.VMEM((N, 16, cols), BF16),

time: 59.1 us -> 57.4 us (0.971)
  the two profiles are of different devices: /device:TPU:99 before, /device:TPU:1 now
where the time goes in v3:
time: 57.4 us; the launch traced here: 57.3 us
  Pallas kernels  54.5 us (95%)
  local copies, waits for them, and re-layouts  2.13 us (4%)
  between operations  0.64 us (1%)
    pallas_call x1, Pallas kernels, local(): pl.pallas_call(kernel, out_shape=(pltpu.VMEM(queries.shape, BF16), pltpu....  54.5 us
    unnamed x3, local copies, waits for them, and re-layouts  2.13 us

profile of v3, /device:TPU:1, one launch (start us, length us, event | category | flops | bytes accessed | tf_op | source)
XLA Modules:
  0.0 57.3 jit_solution(6545152880495306230)
XLA Ops:
  0.6 54.5 %shard_map.94 = (bf16[4,96,1024]{2,1,0:T(8,128)(2,1)S(1)}, bf16[4,96,128]{2,1,0:T(8,128)(2,1)S(1)}, f32[8,640]{1,0:T(8,128)S(1)}) custom-call(bf16[4,96,1024]{2,1,0:T(8,128)(2,1)} %q_hbm.1, bf16[4,96,128]{2,1,0:T(8,128)(2,1)} %k_hbm.1, bf16[4,96,128]{2,1,0:T(8,128)(2,1)} %v_hbm.1, bf16[4,96,640]{2,1,0:T(8,128)(2,1)} %h_hbm.1, bf16[4,96,1024]{2,1,0:T(8,128)(2,1)} %g_hbm.1, ...), custom_call_target="tpu_custom_call" | custom-call | flops 880803840 | bytes 4000000 | tf_op jit(solution)/shard_map/pallas_call | solution.py:390
  55.1 0.9 %copy.13 = bf16[4,96,1024]{2,1,0:T(8,128)(2,1)} copy(bf16[4,96,1024]{2,1,0:T(8,128)(2,1)S(1)} %get-tuple-element.3) | data formatting | bytes 1572864
  56.0 0.6 %copy.15 = f32[8,640]{1,0:T(8,128)} copy(f32[8,640]{1,0:T(8,128)S(1)} %get-tuple-element.5) | data formatting | bytes 40960
  56.6 0.6 %copy.14 = bf16[4,96,128]{2,1,0:T(8,128)(2,1)} copy(bf16[4,96,128]{2,1,0:T(8,128)(2,1)S(1)} %get-tuple-element.4) | data formatting | bytes 196608

commit v4 on v3

--- a/solution.py
+++ b/solution.py
@@ -295,11 +295,11 @@
 
     gathered(0)
     first_sends(0)
-    second_sends(0)
     gathered(1)
     first_sends(1)
+    second_sends(0)
+    second_sends(1)
     last_sends(0)
-    second_sends(1)
     last_sends(1)
     ring_end(0)
     ring_end(1)

time: 57.4 us -> 56.9 us (level)
  no operation moved by 1% of the time
where the time goes in v4:
time: 56.9 us; the launch traced here: 56.8 us
  Pallas kernels  54 us (95%)
  local copies, waits for them, and re-layouts  2.13 us (4%)
  between operations  0.64 us (1%)
    pallas_call x1, Pallas kernels, local(): pl.pallas_call(kernel, out_shape=(pltpu.VMEM(queries.shape, BF16), pltpu....  54 us
    unnamed x3, local copies, waits for them, and re-layouts  2.13 us

profile of v4, /device:TPU:1, one launch (start us, length us, event | category | flops | bytes accessed | tf_op | source)
XLA Modules:
  0.0 56.8 jit_solution(13602473594163859187)
XLA Ops:
  0.6 54.0 %shard_map.94 = (bf16[4,96,1024]{2,1,0:T(8,128)(2,1)S(1)}, bf16[4,96,128]{2,1,0:T(8,128)(2,1)S(1)}, f32[8,640]{1,0:T(8,128)S(1)}) custom-call(bf16[4,96,1024]{2,1,0:T(8,128)(2,1)} %q_hbm.1, bf16[4,96,128]{2,1,0:T(8,128)(2,1)} %k_hbm.1, bf16[4,96,128]{2,1,0:T(8,128)(2,1)} %v_hbm.1, bf16[4,96,640]{2,1,0:T(8,128)(2,1)} %h_hbm.1, bf16[4,96,1024]{2,1,0:T(8,128)(2,1)} %g_hbm.1, ...), custom_call_target="tpu_custom_call" | custom-call | flops 880803840 | bytes 4000000 | tf_op jit(solution)/shard_map/pallas_call | solution.py:390
  54.7 0.9 %copy.13 = bf16[4,96,1024]{2,1,0:T(8,128)(2,1)} copy(bf16[4,96,1024]{2,1,0:T(8,128)(2,1)S(1)} %get-tuple-element.3) | data formatting | bytes 1572864
  55.5 0.6 %copy.15 = f32[8,640]{1,0:T(8,128)} copy(f32[8,640]{1,0:T(8,128)S(1)} %get-tuple-element.5) | data formatting | bytes 40960
  56.1 0.6 %copy.14 = bf16[4,96,128]{2,1,0:T(8,128)(2,1)} copy(bf16[4,96,128]{2,1,0:T(8,128)(2,1)S(1)} %get-tuple-element.4) | data formatting | bytes 196608

commit v5 on v4

--- a/solution.py
+++ b/solution.py
@@ -241,7 +241,6 @@
         for way in (s, 1 - s):
             r_send[way, s, 1] = part[s, way].astype(BF16)
             hop(way, s, 1).start()
-        products(s, (2, -2))
 
     def pass_on(way, s, j):
         total = part[s, way]
@@ -297,6 +296,8 @@
     first_sends(0)
     gathered(1)
     first_sends(1)
+    for s in range(2):
+        products(s, (2, -2))
     second_sends(0)
     second_sends(1)
     last_sends(0)

time: 56.9 us -> 56.9 us (level)
  no operation moved by 1% of the time
where the time goes in v5:
time: 56.9 us; the launch traced here: 56.8 us
  Pallas kernels  54 us (95%)
  local copies, waits for them, and re-layouts  2.13 us (4%)
  between operations  0.64 us (1%)
    pallas_call x1, Pallas kernels, local(): pl.pallas_call(kernel, out_shape=(pltpu.VMEM(queries.shape, BF16), pltpu....  54 us
    unnamed x3, local copies, waits for them, and re-layouts  2.13 us

profile of v5, /device:TPU:1, one launch (start us, length us, event | category | flops | bytes accessed | tf_op | source)
XLA Modules:
  0.0 56.8 jit_solution(12445156274516879128)
XLA Ops:
  0.6 54.0 %shard_map.94 = (bf16[4,96,1024]{2,1,0:T(8,128)(2,1)S(1)}, bf16[4,96,128]{2,1,0:T(8,128)(2,1)S(1)}, f32[8,640]{1,0:T(8,128)S(1)}) custom-call(bf16[4,96,1024]{2,1,0:T(8,128)(2,1)} %q_hbm.1, bf16[4,96,128]{2,1,0:T(8,128)(2,1)} %k_hbm.1, bf16[4,96,128]{2,1,0:T(8,128)(2,1)} %v_hbm.1, bf16[4,96,640]{2,1,0:T(8,128)(2,1)} %h_hbm.1, bf16[4,96,1024]{2,1,0:T(8,128)(2,1)} %g_hbm.1, ...), custom_call_target="tpu_custom_call" | custom-call | flops 880803840 | bytes 4000000 | tf_op jit(solution)/shard_map/pallas_call | solution.py:391
  54.7 0.9 %copy.13 = bf16[4,96,1024]{2,1,0:T(8,128)(2,1)} copy(bf16[4,96,1024]{2,1,0:T(8,128)(2,1)S(1)} %get-tuple-element.3) | data formatting | bytes 1572864
  55.5 0.6 %copy.15 = f32[8,640]{1,0:T(8,128)} copy(f32[8,640]{1,0:T(8,128)S(1)} %get-tuple-element.5) | data formatting | bytes 40960
  56.1 0.6 %copy.14 = bf16[4,96,128]{2,1,0:T(8,128)(2,1)} copy(bf16[4,96,128]{2,1,0:T(8,128)(2,1)S(1)} %get-tuple-element.4) | data formatting | bytes 196608
